TPU v7x, 32 devices: a whole 2x2x4 slice. The times are simulated.
32 devices in a mesh: dp: 16 (over z, x, core), ctx: 2 (over y).
Axes of the slice: x: 2, y: 2, z: 4, core: 2. Of those that a mesh axis runs over, the one named last changes fastest.
Arguments:
- layer_input: bfloat16 [16, 256, 2048], P('dp', 'ctx'), may hold values from -6 to 6
- queries: bfloat16 [16, 256, 2048], P('dp', 'ctx'), may hold values from -26.25 to 26.25
- key_states: bfloat16 [16, 256, 2048], P('dp', 'ctx'), may hold values from -10.5 to 10.5
- value_states: bfloat16 [16, 256, 2048], P('dp', 'ctx'), may hold values from -6 to 6
- out_grad: bfloat16 [16, 256, 2048], P('dp', 'ctx'), may hold values from -6 to 6
- block_kinds: int32 [16, 1], P('dp'), may hold values 0 or 1
Outputs:
- query_grad: bfloat16 [16, 256, 2048], P('dp', 'ctx')
- key_grad: bfloat16 [16, 256, 2048], P('dp', 'ctx')
- value_grad: bfloat16 [16, 256, 2048], P('dp', 'ctx')
- value_weight_gradient: float32 [2048, 2048], P('dp', 'ctx')
Inputs may be any that keep to these rules, and one draw needn't show every extreme that they name: `block_kinds`: 1 marks a frame block of 256 positions, whose positions see each other; 0 marks a text block, causal inside.
All inputs are finite; a program needn't handle non-finite values.
Results may differ from a plain program's by a relative error of at most 0.012.
Values may be sent and summed in bfloat16 or wider, within the bound.
A program may use at most 64 MiB of HBM per device.

v0:
```python
import jax
import jax.numpy as jnp
from jax import lax
from jax.sharding import PartitionSpec as P

FRAME = 256
HEAD_DIM = 128
D_IN = 2048


NEG_FILL = -1e30


def tile_scores(query_tile, key_block):
    product = jnp.einsum("ihd,jhd->hij", query_tile, key_block, preferred_element_type=jnp.float32)
    return product * HEAD_DIM ** (-0.5)


def tile_mask(row_start, key_start, key_count, block_kinds):
    query_pos = row_start + lax.iota(jnp.int32, FRAME)
    key_positions = key_start + lax.iota(jnp.int32, key_count)
    frame_flag = lax.dynamic_index_in_dim(block_kinds, row_start // FRAME, keepdims=False) == 1
    same_block = (key_positions // FRAME)[None, :] == (query_pos // FRAME)[:, None]
    return ((key_positions[None, :] <= query_pos[:, None]) | same_block & frame_flag)[None]


def rows_of(complete_rows, tile_index):
    return lax.dynamic_slice_in_dim(complete_rows, tile_index * FRAME, FRAME, 0)


def cols_of(stat_rows, tile_index):
    return lax.dynamic_slice_in_dim(stat_rows, tile_index * FRAME, FRAME, 1)


def put_cols(stat_rows, new_part, tile_index):
    return lax.dynamic_update_slice_in_dim(stat_rows, new_part, tile_index * FRAME, 1)


def head_split(stat_rows, work_items):
    pieces_out = []
    for work_item in work_items:
        pieces_out.append(stat_rows)
    return pieces_out


def sweep_peak(work_item, block_kinds):
    query_h, grad_h, key_block, value_block, key_start = work_item

    def advance(tile_index, peak_now):
        attention_scores = tile_scores(rows_of(query_h, tile_index), key_block)
        allowed = tile_mask(tile_index * FRAME, key_start, key_block.shape[0], block_kinds)
        return put_cols(
            peak_now, jnp.max(jnp.where(allowed, attention_scores, NEG_FILL), axis=2), tile_index
        )

    start_value = jnp.full((key_block.shape[1], query_h.shape[0]), NEG_FILL, jnp.float32)
    return lax.fori_loop(key_start // FRAME, query_h.shape[0] // FRAME, advance, start_value)


def sweep_total(work_item, block_kinds, peak_rows):
    query_h, grad_h, key_block, value_block, key_start = work_item

    def advance(tile_index, total_now):
        attention_scores = tile_scores(rows_of(query_h, tile_index), key_block)
        allowed = tile_mask(tile_index * FRAME, key_start, key_block.shape[0], block_kinds)
        shifted = jnp.exp(attention_scores - cols_of(peak_rows, tile_index)[:, :, None])
        return put_cols(total_now, jnp.sum(jnp.where(allowed, shifted, 0.0), axis=2), tile_index)

    start_value = jnp.zeros((key_block.shape[1], query_h.shape[0]), jnp.float32)
    return lax.fori_loop(key_start // FRAME, query_h.shape[0] // FRAME, advance, start_value)


def sweep_delta(work_item, block_kinds, log_rows):
    query_h, grad_h, key_block, value_block, key_start = work_item

    def advance(tile_index, delta_now):
        attention_scores = tile_scores(rows_of(query_h, tile_index), key_block)
        allowed = tile_mask(tile_index * FRAME, key_start, key_block.shape[0], block_kinds)
        weights = jnp.where(
            allowed, jnp.exp(attention_scores - cols_of(log_rows, tile_index)[:, :, None]), 0.0
        )
        grad_probs = jnp.einsum(
            "ihd,jhd->hij",
            rows_of(grad_h, tile_index),
            value_block,
            preferred_element_type=jnp.float32,
        )
        return put_cols(delta_now, jnp.sum(weights * grad_probs, axis=2), tile_index)

    start_value = jnp.zeros((key_block.shape[1], query_h.shape[0]), jnp.float32)
    return lax.fori_loop(key_start // FRAME, query_h.shape[0] // FRAME, advance, start_value)


def sweep_grads(work_item, block_kinds, log_rows, delta_rows):
    query_h, grad_h, key_block, value_block, key_start = work_item
    score_scale = HEAD_DIM ** (-0.5)

    def advance(tile_index, carry):
        key_acc, value_acc, dq_term = carry
        query_tile = rows_of(query_h, tile_index)
        gradient_piece = rows_of(grad_h, tile_index)
        attention_scores = tile_scores(query_tile, key_block)
        allowed = tile_mask(tile_index * FRAME, key_start, key_block.shape[0], block_kinds)
        weights = jnp.where(
            allowed, jnp.exp(attention_scores - cols_of(log_rows, tile_index)[:, :, None]), 0.0
        )
        grad_probs = jnp.einsum(
            "ihd,jhd->hij", gradient_piece, value_block, preferred_element_type=jnp.float32
        )
        grad_scores = (
            weights * (grad_probs - cols_of(delta_rows, tile_index)[:, :, None]) * score_scale
        ).astype(jnp.bfloat16)
        weights_half = weights.astype(jnp.bfloat16)
        value_acc = value_acc + jnp.einsum(
            "hij,ihd->jhd", weights_half, gradient_piece, preferred_element_type=jnp.float32
        )
        key_acc = key_acc + jnp.einsum(
            "hij,ihd->jhd", grad_scores, query_tile, preferred_element_type=jnp.float32
        )
        query_rows_part = jnp.einsum(
            "hij,jhd->ihd", grad_scores, key_block, preferred_element_type=jnp.float32
        )
        dq_term = lax.dynamic_update_slice_in_dim(dq_term, query_rows_part, tile_index * FRAME, 0)
        return (key_acc, value_acc, dq_term)

    start_value = (
        jnp.zeros(key_block.shape, jnp.float32),
        jnp.zeros(key_block.shape, jnp.float32),
        jnp.zeros(query_h.shape, jnp.float32),
    )
    return lax.fori_loop(key_start // FRAME, query_h.shape[0] // FRAME, advance, start_value)


def body(layer_input, queries, key_states, value_states, out_grad, block_kinds):
    shard_rows = queries.shape[1]
    row_width = queries.shape[2]
    head_count = row_width // HEAD_DIM
    ctx_size = lax.axis_size("ctx")
    dp_size = lax.axis_size("dp")
    my_index = lax.axis_index("ctx")
    kinds_row = block_kinds[0]
    query_all, grad_all = (
        lax.all_gather(queries[0], "ctx", axis=0, tiled=True),
        lax.all_gather(out_grad[0], "ctx", axis=0, tiled=True),
    )
    total_rows = query_all.shape[0]
    query_all = query_all.reshape(total_rows, head_count, HEAD_DIM)
    grad_all = grad_all.reshape(total_rows, head_count, HEAD_DIM)
    own_keys = key_states[0].reshape(shard_rows, head_count, HEAD_DIM)
    own_values = value_states[0].reshape(shard_rows, head_count, HEAD_DIM)
    own_start = my_index * shard_rows
    work_items = [(query_all, grad_all, own_keys, own_values, own_start)]
    row_peaks = jnp.concatenate(
        [sweep_peak(work_item, kinds_row) for work_item in work_items], axis=0
    )
    row_peaks = lax.pmax(row_peaks.astype(jnp.bfloat16), "ctx").astype(row_peaks.dtype)
    peak_parts = head_split(row_peaks, work_items)
    totals = jnp.concatenate(
        [
            sweep_total(work_item, kinds_row, peak_part)
            for work_item, peak_part in zip(work_items, peak_parts)
        ],
        axis=0,
    )
    totals = lax.psum(totals, "ctx")
    log_total = row_peaks + jnp.log(totals)
    log_parts = head_split(log_total, work_items)
    deltas = jnp.concatenate(
        [
            sweep_delta(work_item, kinds_row, log_part)
            for work_item, log_part in zip(work_items, log_parts)
        ],
        axis=0,
    )
    deltas = lax.psum(deltas, "ctx")
    delta_parts = head_split(deltas, work_items)
    results = [
        sweep_grads(work_item, kinds_row, log_part, delta_part)
        for work_item, log_part, delta_part in zip(work_items, log_parts, delta_parts)
    ]
    dq_term = jnp.concatenate([entry_set[2] for entry_set in results], axis=1).reshape(
        total_rows, row_width
    )
    query_grad = lax.psum_scatter(
        dq_term.astype(jnp.bfloat16), "ctx", scatter_dimension=0, tiled=True
    )
    key_grad = results[0][0].astype(jnp.bfloat16)
    value_grad = results[0][1].astype(jnp.bfloat16)
    key_grad = key_grad.reshape(shard_rows, row_width)
    value_grad = value_grad.reshape(shard_rows, row_width)
    rows_each = D_IN // dp_size
    cols_each = row_width // ctx_size
    divided_input = layer_input[0].reshape(shard_rows, dp_size, rows_each)
    divided_gradient = value_grad.reshape(shard_rows, ctx_size, cols_each)
    weight_term = jnp.einsum(
        "zkg,zbi->kbgi", divided_input, divided_gradient, preferred_element_type=jnp.float32
    )
    weight_term = weight_term.reshape(dp_size * ctx_size * rows_each, cols_each)
    weight_grad = lax.psum_scatter(weight_term, ("dp", "ctx"), scatter_dimension=0, tiled=True)
    return (query_grad[None], key_grad[None], value_grad[None], weight_grad)


def solution(mesh):
    return jax.shard_map(
        body,
        mesh=mesh,
        in_specs=(
            P("dp", "ctx", None),
            P("dp", "ctx", None),
            P("dp", "ctx", None),
            P("dp", "ctx", None),
            P("dp", "ctx", None),
            P("dp", None),
        ),
        out_specs=(
            P("dp", "ctx", None),
            P("dp", "ctx", None),
            P("dp", "ctx", None),
            P("dp", "ctx"),
        ),
        check_vma=False,
    )
```

profile of v0, /device:TPU:0, one launch (start us, length us, event | category | flops | bytes accessed | tf_op | source)
XLA Modules:
  0.0 471.0 jit_solution(11475224542814934308)
XLA Ops:
  7.2 2.1 copy.18
  9.4 2.1 copy.24
  13.4 20.8 %all-gather.5.cloned.1.call-done = bf16[1,256,2048]{1,2,0:T(8,128)(2,1)} async-done(((bf16[1,128,2048]{1,2,0:T(8,128)(2,1)}), bf16[1,256,2048]{1,2,0:T(8,128)(2,1)}) %all-gather.5.cloned.1.call-update) | async-done | bytes 1048592 | tf_op jit(solution)/shard_map/all_gather | solution.py:143
  34.1 1.6 copy.30
  36.3 1.2 while.56
  36.5 1.1 select_reduce_fusion.4
  37.6 5.1 %pmax.7 = bf16[16,256]{1,0:T(8,128)(2,1)S(1)} all-reduce(bf16[16,256]{1,0:T(8,128)(2,1)} %get-tuple-element.534), channel_id=1, replica_groups=mesh['dp'=16,'ctx'=2] {'ctx'}, use_global_device_ids=true, to_apply=%region_3.4 | all-reduce | flops 4096 | bytes 16384 | tf_op jit(solution)/shard_map/pmax | solution.py:156
  43.3 1.4 while.57
  43.4 1.3 select_reduce_fusion.5
  44.7 7.9 %psum.14 = f32[16,256]{1,0:T(8,128)S(1)} all-reduce(f32[16,256]{1,0:T(8,128)} %get-tuple-element.535), channel_id=1, replica_groups=mesh['dp'=16,'ctx'=2] {'ctx'}, use_global_device_ids=true, to_apply=%region_7.8 | all-reduce | flops 4096 | bytes 32768 | tf_op jit(solution)/shard_map/psum | solution.py:165
  52.6 5.3 %all-gather.7.cloned.1.call-done = bf16[1,256,2048]{1,2,0:T(8,128)(2,1)} async-done(((bf16[1,128,2048]{1,2,0:T(8,128)(2,1)}), bf16[1,256,2048]{1,2,0:T(8,128)(2,1)}) %all-gather.7.cloned.1.call-update) | async-done | bytes 1048592 | tf_op jit(solution)/shard_map/all_gather | solution.py:144
  57.9 1.6 copy.32
  60.1 1.9 while.58
  60.7 1.3 multiply_reduce_fusion.2
  62.0 7.6 %psum.15 = f32[16,256]{1,0:T(8,128)S(1)} all-reduce(f32[16,256]{1,0:T(8,128)} %get-tuple-element.536), channel_id=1, replica_groups=mesh['dp'=16,'ctx'=2] {'ctx'}, use_global_device_ids=true, to_apply=%region_11.12 | all-reduce | flops 4096 | bytes 32768 | tf_op jit(solution)/shard_map/psum | solution.py:175
  69.6 1.1 broadcast.859.clone
  70.7 1.2 broadcast_in_dim.105
  71.9 1.1 broadcast.859
  73.0 7.1 %while.59 = (s32[]{:T(128)}, f32[128,16,128]{2,0,1:T(8,128)}, f32[128,16,128]{2,0,1:T(8,128)}, bf16[256,16,128]{2,0,1:T(8,128)(2,1)}, s32[]{:T(128)}, /*index=5*...) while((s32[]{:T(128)}, f32[128,16,128]{2,0,1:T(8,128)}, ...), condition=%wide.region_13.14_spmd, body=%wide.region_12.13_spmd.sunk | while | flops 675944448 | bytes 37329160 | solution.py:131
  73.2 1.0 exponential_select_fusion.2
  74.2 0.8 multiply_convert_fusion.2
  75.5 0.8 fusion.65
  76.3 1.5 convolution_bitcast_fusion.5
  78.2 0.8 fusion.64
  79.1 1.0 copy-done.4
  80.1 2.5 copy_bitcast_fusion
  83.4 2.3 convolution_bitcast_fusion.3
  85.8 6.5 %copy.39 = f32[16,2,128,1024]{3,2,1,0:T(8,128)} copy(f32[16,2,128,1024]{3,2,0,1:T(8,128)S(1)} %convolution_bitcast_fusion.3) | data formatting | bytes 33554432 | tf_op jit(solution)/shard_map/zkg,zbi->kbgi/transpose | solution.py:195
  92.3 1.0 copy.40
  94.1 1.0 broadcast_in_dim_reshape.6
  95.1 9.1 %reduce-scatter.3.cloned.1.call-done = bf16[128,2048]{1,0:T(8,128)(2,1)} async-done(((bf16[256,2048]{1,0:T(8,128)(2,1)}), bf16[128,2048]{1,0:T(8,128)(2,1)}) %reduce-scatter.3.cloned.1.call-update) | async-done | bytes 524304 | tf_op jit(solution)/shard_map/reduce_scatter | solution.py:184
  104.2 360.2 %reduce-scatter.5.cloned.1.call-done = f32[128,1024]{1,0:T(8,128)} async-done(((f32[4096,1024]{1,0:T(8,128)}), f32[128,1024]{1,0:T(8,128)}) %reduce-scatter.5.cloned.1.call-update) | async-done | bytes 524304 | tf_op jit(solution)/shard_map/reduce_scatter | solution.py:199
  (51 shorter events, 6.6 us)
Async XLA Ops:
  7.2 5.0 %copy-start.6 = (bf16[1,128,2048]{2,1,0:T(8,128)(2,1)S(1)}, bf16[1,128,2048]{2,1,0:T(8,128)(2,1)}, u32[]{:S(2)}) copy-start(bf16[1,128,2048]{2,1,0:T(8,128)(2,1)} %param.16) | copy-start | bytes 1572868
  7.2 27.0 %all-gather.5.cloned.1.call-start = ((), (), s32[]{:S(2)}) async-start(), calls=%async_computation.4 | async-start | bytes 1572864 | tf_op jit(solution)/shard_map/all_gather | solution.py:143
  9.3 3.5 copy-start.7
  9.3 48.6 %all-gather.7.cloned.1.call-start = ((), (), s32[]{:S(2)}) async-start(), calls=%async_computation.5 | async-start | bytes 1572864 | tf_op jit(solution)/shard_map/all_gather | solution.py:144
  11.5 92.7 %reduce-scatter.3.cloned.1.call-start = ((), (), s32[]{:S(2)}) async-start(), calls=%async_computation.2 | async-start | bytes 1572864 | tf_op jit(solution)/shard_map/reduce_scatter | solution.py:184
  74.2 1.2 copy-start
  76.2 2.8 copy-start.1
  76.3 2.0 copy-start.3
  79.1 1.0 copy-start.4
  80.1 2.8 copy-start.8
  80.1 3.1 copy-start.2
  82.6 381.8 %reduce-scatter.5.cloned.1.call-start = ((), (), s32[]{:S(2)}) async-start(), calls=%async_computation.3 | async-start | bytes 17301504 | tf_op jit(solution)/shard_map/reduce_scatter | solution.py:199
  92.3 1.4 copy-start.5
Sparse Core Ops, SparseCore 0:
  10.1 23.9 all-gather.4
  36.2 21.6 all-gather.6
  82.7 21.4 reduce-scatter.2
  107.1 357.3 reduce-scatter.4
where the time goes:
time: 471 us
  waiting for transfers between devices  395 us (84%)
  local copies, waits for them, and re-layouts  27.9 us (6%)
  blocking collectives  20.6 us (4%)
  between operations  14.5 us (3%)
  matrix products  11.3 us (2%)
    reduce_scatter x1, waiting for transfers between devices, body(): lax.psum_scatter(weight_term, ('dp', 'ctx'), scatter_dimension=0, tiled=T...  360 us
    all_gather x1, waiting for transfers between devices, body(): lax.all_gather(queries[0], 'ctx', axis=0, tiled=True)  20.8 us
  transfers between devices with their start and end apart: 4, of which 4 were waited for; matrix products, arithmetic and copies ran while one was open for 4% of the time, Pallas kernels for 0%

commit v1 on v0

--- a/solution.py
+++ b/solution.py
@@ -1,6 +1,10 @@
+import functools
+
 import jax
 import jax.numpy as jnp
 from jax import lax
+from jax.experimental import pallas as pl
+from jax.experimental.pallas import tpu as pltpu
 from jax.sharding import PartitionSpec as P
 
 FRAME = 256
@@ -200,9 +204,378 @@
     return (query_grad[None], key_grad[None], value_grad[None], weight_grad)
 
 
+HEADS_PER_CHUNK = 2
+CHUNK = HEADS_PER_CHUNK * HEAD_DIM
+MESH = pl.DeviceIdType.MESH
+F32 = jnp.float32
+BF16 = jnp.bfloat16
+SCALE = HEAD_DIM ** (-0.5)
+PLANE = [(dx, dc, dy) for dx in (0, 1) for dc in (0, 1) for dy in (0, 1)]
+
+
+def dot_last(a, b):
+    return lax.dot_general(a, b, (((1,), (1,)), ((), ())), preferred_element_type=F32)
+
+
+def dot_first(a, b):
+    return lax.dot_general(a, b, (((0,), (0,)), ((), ())), preferred_element_type=F32)
+
+
+def dot_plain(a, b):
+    return lax.dot_general(a, b, (((1,), (0,)), ((), ())), preferred_element_type=F32)
+
+
+def fused_kernel(
+    sizes,
+    kinds,
+    x_in,
+    q_in,
+    k_in,
+    v_in,
+    g_in,
+    dq_out,
+    dk_out,
+    dv_out,
+    w_out,
+    qkvg,
+    dq_s,
+    dk_s,
+    vall,
+    lall,
+    lt,
+    w_send,
+    w_recv,
+    w_own,
+    in_send,
+    in_recv,
+    in_local,
+    l_send,
+    l_recv,
+    l_local,
+    v_send,
+    v_recv,
+    r_send,
+    r_recv,
+    o_local,
+    z_send,
+    z_recv,
+    w_local,
+):
+    rows, half, nz, chunks = sizes
+    seq = 2 * rows
+    each = HEAD_DIM
+    dp = lax.axis_index("dp")
+    y = lax.axis_index("ctx")
+    c = lax.rem(dp, 2)
+    x = lax.rem(dp // 2, 2)
+    z = dp // 4
+    yp = 1 - y
+
+    def plane_id(dx, dc, dy):
+        xx = lax.rem(x + dx, 2)
+        cc = lax.rem(c + dc, 2)
+        yy = lax.rem(y + dy, 2)
+        return ((z * 2 + xx) * 2 + cc, yy), xx, cc
+
+    def z_id(dz):
+        return (lax.rem(z + dz, nz) * 4 + x * 2 + c, y)
+
+    barrier = pltpu.get_barrier_semaphore()
+    for dx, dc, dy in PLANE[1:]:
+        pl.semaphore_signal(barrier, inc=1, device_id=plane_id(dx, dc, dy)[0], device_id_type=MESH)
+    for dz in range(1, nz):
+        pl.semaphore_signal(barrier, inc=1, device_id=z_id(dz), device_id_type=MESH)
+
+    def aligned(value):
+        return pl.multiple_of(value, 128)
+
+    my_rows = pl.ds(aligned(y * rows), rows)
+    peer_rows = pl.ds(aligned(yp * rows), rows)
+
+    def remote(src, dst, send_sem, recv_sem, device):
+        return pltpu.make_async_remote_copy(
+            src_ref=src,
+            dst_ref=dst,
+            send_sem=send_sem,
+            recv_sem=recv_sem,
+            device_id=device,
+            device_id_type=MESH,
+        )
+
+    sources = (q_in, k_in, v_in, g_in)
+    local_in = []
+    for n in range(chunks):
+        cols = pl.ds(n * CHUNK, CHUNK)
+        mine = pl.ds(aligned(y * half + n * CHUNK), CHUNK)
+        local_in.append(
+            [
+                pltpu.make_async_copy(
+                    src.at[:, mine], qkvg.at[t, my_rows, cols], in_local.at[n, t]
+                )
+                for t, src in enumerate(sources)
+            ]
+        )
+    for copies in local_in:
+        for copy in copies:
+            copy.start()
+    l_own = []
+    for dz in range(nz):
+        col = pl.ds(aligned((lax.rem(z + dz, nz) * 4 + x * 2 + c) * each), each)
+        l_own.append(
+            pltpu.make_async_copy(
+                x_in.at[:, col], lall.at[my_rows, pl.ds(dz * each, each)], l_local.at[dz]
+            )
+        )
+        l_own[-1].start()
+
+    pl.semaphore_wait(barrier, 7 + nz - 1)
+
+    peer_id = plane_id(0, 0, 1)[0]
+    sends_in = []
+    for n in range(chunks):
+        cols = pl.ds(n * CHUNK, CHUNK)
+        theirs = pl.ds(aligned(yp * half + n * CHUNK), CHUNK)
+        sends_in.append(
+            [
+                remote(
+                    src.at[:, theirs],
+                    qkvg.at[t, my_rows, cols],
+                    in_send.at[n, t],
+                    in_recv.at[n, t],
+                    peer_id,
+                )
+                for t, src in enumerate(sources)
+            ]
+        )
+    sends_l = []
+    for p, (dx, dc, dy) in enumerate(PLANE):
+        if p == 0:
+            continue
+        device, xx, cc = plane_id(dx, dc, dy)
+        slot = dx * 2 + dc
+        dst_rows = pl.ds(aligned(slot * seq + y * rows), rows)
+        for dz in range(nz):
+            col = pl.ds(aligned((lax.rem(z + dz, nz) * 4 + xx * 2 + cc) * each), each)
+            sends_l.append(
+                remote(
+                    x_in.at[:, col],
+                    lall.at[dst_rows, pl.ds(dz * each, each)],
+                    l_send.at[p - 1, dz],
+                    l_recv.at[p - 1, dz],
+                    device,
+                )
+            )
+    for n in range(chunks):
+        for copy in sends_in[n]:
+            copy.start()
+        if n == 0:
+            for copy in sends_l:
+                copy.start()
+
+    key_pos = lax.broadcasted_iota(jnp.int32, (seq, seq), 0)
+    query_pos = lax.broadcasted_iota(jnp.int32, (seq, seq), 1)
+    allowed = key_pos <= query_pos + kinds[0, 0] * seq
+
+    def head(h):
+        hc = pl.ds(h * HEAD_DIM, HEAD_DIM)
+        q = qkvg[0, :, hc]
+        k = qkvg[1, :, hc]
+        v = qkvg[2, :, hc]
+        g = qkvg[3, :, hc]
+        scores = jnp.where(allowed, dot_last(k, q) * SCALE, NEG_FILL)
+        peak = jnp.max(scores, axis=0, keepdims=True)
+        p = jnp.exp(scores - peak)
+        weights = p * (1.0 / jnp.sum(p, axis=0, keepdims=True))
+        weights_half = weights.astype(BF16)
+        vall[pl.ds(0, seq), hc] = dot_plain(weights_half, g).astype(BF16)
+        grad_probs = dot_last(v, g)
+        delta = jnp.sum(weights * grad_probs, axis=0, keepdims=True)
+        grad_scores = (weights * (grad_probs - delta) * SCALE).astype(BF16)
+        dk_s[:, hc] = dot_plain(grad_scores, q).astype(BF16)
+        parts = [
+            dot_first(grad_scores[s * rows : (s + 1) * rows], k[s * rows : (s + 1) * rows])
+            .astype(BF16)
+            .astype(F32)
+            for s in range(2)
+        ]
+        dq_s[:, hc] = (parts[0] + parts[1]).astype(BF16)
+
+    v_copies, r_copies, z_copies, o_copies = [], [], [], []
+
+    def attention(n):
+        for t in range(4):
+            local_in[n][t].wait()
+            sends_in[n][t].wait_recv()
+        for j in range(HEADS_PER_CHUNK):
+            head(n * HEADS_PER_CHUNK + j)
+        cols = pl.ds(n * CHUNK, CHUNK)
+        group = []
+        for slot in (2, 3, 1):
+            group.append(
+                remote(
+                    vall.at[pl.ds(0, seq), cols],
+                    vall.at[pl.ds(slot * seq, seq), cols],
+                    v_send.at[n, slot - 1],
+                    v_recv.at[n, slot - 1],
+                    plane_id(slot // 2, slot % 2, 0)[0],
+                )
+            )
+            group[-1].start()
+        v_copies.append(group)
+        out_cols = pl.ds(aligned(y * half + n * CHUNK), CHUNK)
+        results = ((vall, dv_out), (dk_s, dk_out), (dq_s, dq_out))
+        group = []
+        for t, (src, dst) in enumerate(results):
+            group.append(
+                remote(
+                    src.at[peer_rows, cols],
+                    dst.at[:, out_cols],
+                    r_send.at[n, t],
+                    r_recv.at[n, t],
+                    peer_id,
+                )
+            )
+            group[-1].start()
+        r_copies.append(group)
+        group = []
+        for t, (src, dst) in enumerate(results):
+            group.append(
+                pltpu.make_async_copy(
+                    src.at[my_rows, cols], dst.at[:, out_cols], o_local.at[n, t]
+                )
+            )
+            group[-1].start()
+        o_copies.append(group)
+
+    def weight(n):
+        for copy in v_copies[n]:
+            copy.wait_recv()
+        cols = pl.ds(n * CHUNK, CHUNK)
+        term = dot_plain(lt[...], vall[:, cols])
+        w_own[:, cols] = term[:each]
+        group = []
+        for dz in range(1, nz):
+            w_send[dz - 1, :, cols] = term[dz * each : (dz + 1) * each].astype(BF16)
+            group.append(
+                remote(
+                    w_send.at[dz - 1, :, cols],
+                    w_recv.at[dz - 1, :, cols],
+                    z_send.at[n, dz - 1],
+                    z_recv.at[n, dz - 1],
+                    z_id(dz),
+                )
+            )
+            group[-1].start()
+        z_copies.append(group)
+
+    attention(0)
+    for n in range(1, chunks):
+        attention(n)
+        if n == 1:
+            for copy in l_own:
+                copy.wait()
+            for copy in sends_l:
+                copy.wait_recv()
+            for s in range(4):
+                lt[:, pl.ds(s * seq, seq)] = lall[pl.ds(s * seq, seq), :].T
+        weight(n - 1)
+    weight(chunks - 1)
+
+    w_copies = []
+    for n in range(chunks):
+        cols = pl.ds(n * CHUNK, CHUNK)
+        total = w_own[:, cols]
+        for dz in range(1, nz):
+            z_copies[n][dz - 1].wait_recv()
+            total = total + w_recv[dz - 1, :, cols].astype(F32)
+        w_own[:, cols] = total
+        w_copies.append(
+            pltpu.make_async_copy(w_own.at[:, cols], w_out.at[:, cols], w_local.at[n])
+        )
+        w_copies[-1].start()
+
+    for copies in sends_in + v_copies + z_copies + [sends_l]:
+        for copy in copies:
+            copy.wait_send()
+    for copies in r_copies + o_copies + [w_copies]:
+        for copy in copies:
+            copy.wait()
+
+
+def fused_body(layer_input, queries, key_states, value_states, out_grad, block_kinds):
+    rows, width = queries.shape[1:]
+    half = width // 2
+    nz = lax.axis_size("dp") // 4
+    chunks = half // CHUNK
+    seq = 2 * rows
+    depth = 4 * seq
+    each = HEAD_DIM
+    dma = pltpu.SemaphoreType.DMA
+    half_out = jax.ShapeDtypeStruct((rows, width), BF16)
+    outs = pl.pallas_call(
+        functools.partial(fused_kernel, (rows, half, nz, chunks)),
+        out_shape=(half_out, half_out, half_out, jax.ShapeDtypeStruct((each, half), F32)),
+        in_specs=[pl.BlockSpec(memory_space=pltpu.SMEM)]
+        + [pl.BlockSpec(memory_space=pl.ANY)] * 5,
+        out_specs=[pl.BlockSpec(memory_space=pl.ANY)] * 4,
+        scratch_shapes=[
+            pltpu.VMEM((4, seq, half), BF16),
+            pltpu.VMEM((seq, half), BF16),
+            pltpu.VMEM((seq, half), BF16),
+            pltpu.VMEM((depth, half), BF16),
+            pltpu.VMEM((depth, nz * each), BF16),
+            pltpu.VMEM((nz * each, depth), BF16),
+            pltpu.VMEM((nz - 1, each, half), BF16),
+            pltpu.VMEM((nz - 1, each, half), BF16),
+            pltpu.VMEM((each, half), F32),
+            dma((chunks, 4)),
+            dma((chunks, 4)),
+            dma((chunks, 4)),
+            dma((7, nz)),
+            dma((7, nz)),
+            dma((nz,)),
+            dma((chunks, 3)),
+            dma((chunks, 3)),
+            dma((chunks, 3)),
+            dma((chunks, 3)),
+            dma((chunks, 3)),
+            dma((chunks, nz - 1)),
+            dma((chunks, nz - 1)),
+            dma((chunks,)),
+        ],
+        compiler_params=pltpu.CompilerParams(
+            collective_id=0, has_side_effects=True, vmem_limit_bytes=48 * 1024 * 1024
+        ),
+        cost_estimate=pl.CostEstimate(
+            flops=2 * (5 * seq * seq * half + depth * nz * each * half),
+            bytes_accessed=8 * rows * width * 2 + each * half * 4,
+            transcendentals=seq * seq * half // HEAD_DIM,
+        ),
+    )(block_kinds, layer_input[0], queries[0], key_states[0], value_states[0], out_grad[0])
+    return (outs[0][None], outs[1][None], outs[2][None], outs[3])
+
+
+def pick_body(mesh):
+    ctx_size, dp_size = mesh.shape["ctx"], mesh.shape["dp"]
+
+    def chosen(layer_input, queries, *others):
+        fits = (
+            ctx_size == 2
+            and dp_size % 4 == 0
+            and dp_size > 4
+            and dp_size * HEAD_DIM == D_IN
+            and queries.shape[0] == 1
+            and 2 * queries.shape[1] == FRAME
+            and queries.shape[2] % (2 * CHUNK) == 0
+        )
+        return (fused_body if fits else body)(layer_input, queries, *others)
+
+    return chosen
+
+
 def solution(mesh):
     return jax.shard_map(
-        body,
+        pick_body(mesh),
         mesh=mesh,
         in_specs=(
             P("dp", "ctx", None),

time: 471 us -> 69.4 us (0.15)
  waiting for transfers between devices: 395 us -> 0 us
  Pallas kernels: 0 us -> 59.3 us
  blocking collectives: 20.6 us -> 0 us
  local copies, waits for them, and re-layouts: 27.9 us -> 8.37 us
  between operations: 14.5 us -> 1.3 us
  matrix products: 11.3 us -> 0 us
    reduce_scatter x2 -> x0, waiting for transfers between devices: 369 us -> none  [the longest x1 360 us: body(): lax.psum_scatter(weight_term, ('dp', 'ctx'), scatter_dimension=0, tiled=T...]
    pallas_call x0 -> x1, Pallas kernels: none -> 59.3 us  [fused_body(): pl.pallas_call(functools.partial(fused_kernel, (rows, half, nz, chunks)),...]
    all_gather x2 -> x0, waiting for transfers between devices: 26 us -> none  [the longest x1 20.8 us: body(): lax.all_gather(queries[0], 'ctx', axis=0, tiled=True)]
    psum x2 -> x0, blocking collectives: 15.5 us -> none  [the longest x1 7.9 us: body(): totals = lax.psum(totals, 'ctx')]
    dot_general x10 -> x0, matrix products: 11.3 us -> none  [the longest x4 3.81 us: tile_scores(): jnp.einsum('ihd,jhd->hij', query_tile, key_block, preferred_element_type=...]
    transpose x1 -> x0, local copies, waits for them, and re-layouts: 6.54 us -> none  [body(): jnp.einsum('zkg,zbi->kbgi', divided_input, divided_gradient, preferred_el...]
    while x13 -> x0, local copies, waits for them, and re-layouts: 5.96 us -> none  [the longest x5 4.07 us: sweep_grads(): lax.fori_loop(key_start // FRAME, query_h.shape[0] // FRAME, advance, sta...]
    pmax x1 -> x0, blocking collectives: 5.1 us -> none  [body(): lax.pmax(row_peaks.astype(jnp.bfloat16), 'ctx').astype(row_peaks.dtype)]
  transfers between devices with their start and end apart: 4 -> 0, of which waited for: 4 -> 0; matrix products, arithmetic and copies ran while one was open for 4% -> 0% of each run, Pallas kernels for 0% -> 0%
where the time goes in v1:
time: 69.4 us; the launch traced here: 69 us
  Pallas kernels  59.3 us (85%)
  local copies, waits for them, and re-layouts  8.37 us (12%)
  between operations  1.3 us (2%)
    pallas_call x1, Pallas kernels, fused_body(): pl.pallas_call(functools.partial(fused_kernel, (rows, half, nz, chunks)),...  59.3 us
    unnamed x14, local copies, waits for them, and re-layouts  8.37 us

profile of v1, /device:TPU:0, one launch (start us, length us, event | category | flops | bytes accessed | tf_op | source)
XLA Modules:
  0.0 69.0 jit_solution(3023420967326192972)
XLA Ops:
  1.3 0.0 copy-start
  1.3 1.0 %copy-done = bf16[1,128,2048]{2,1,0:T(8,128)(2,1)S(1)} copy-done((bf16[1,128,2048]{2,1,0:T(8,128)(2,1)S(1)}, bf16[1,128,2048]{2,1,0:T(8,128)(2,1)}, u32[]{:S(2)}) %copy-start) | copy-done | bytes 524312
  2.3 0.0 copy-start.1
  2.3 1.0 %copy-done.1 = bf16[1,128,2048]{2,1,0:T(8,128)(2,1)S(1)} copy-done((bf16[1,128,2048]{2,1,0:T(8,128)(2,1)S(1)}, bf16[1,128,2048]{2,1,0:T(8,128)(2,1)}, u32[]{:S(2)}) %copy-start.1) | copy-done | bytes 524312
  3.4 0.0 copy-start.2
  3.4 1.0 %copy-done.2 = bf16[1,128,2048]{2,1,0:T(8,128)(2,1)S(1)} copy-done((bf16[1,128,2048]{2,1,0:T(8,128)(2,1)S(1)}, bf16[1,128,2048]{2,1,0:T(8,128)(2,1)}, u32[]{:S(2)}) %copy-start.2) | copy-done | bytes 524312
  4.4 0.0 copy-start.3
  4.4 1.0 %copy-done.3 = bf16[1,128,2048]{2,1,0:T(8,128)(2,1)S(1)} copy-done((bf16[1,128,2048]{2,1,0:T(8,128)(2,1)S(1)}, bf16[1,128,2048]{2,1,0:T(8,128)(2,1)}, u32[]{:S(2)}) %copy-start.3) | copy-done | bytes 524312
  5.4 0.0 copy-start.4
  5.5 1.0 %copy-done.4 = bf16[1,128,2048]{2,1,0:T(8,128)(2,1)S(1)} copy-done((bf16[1,128,2048]{2,1,0:T(8,128)(2,1)S(1)}, bf16[1,128,2048]{2,1,0:T(8,128)(2,1)}, u32[]{:S(2)}) %copy-start.4) | copy-done | bytes 524312
  6.5 59.3 %shard_map.93 = (bf16[128,2048]{1,0:T(8,128)(2,1)S(1)}, bf16[128,2048]{1,0:T(8,128)(2,1)S(1)}, bf16[128,2048]{1,0:T(8,128)(2,1)S(1)}, f32[128,1024]{1,0:T(8,128)S(1)}) custom-call(s32[1,1]{1,0:T(1,128)S(6)} %copy.14.kinds, bf16[128,2048]{1,0:T(8,128)(2,1)S(1)} %bitcast.11, bf16[128,2048]{1,0:T(8,128)(2,1)S(1)} %bitcast.12, bf16[128,2048]{1,0:T(8,128)(2,1)S(1)} %bitcast.13, ...), custom_call_target="tpu_custom_call" | custom-call | flops 1744830464 | bytes 4718592 | tf_op jit(solution)/shard_map/pallas_call | solution.py:515
  65.8 0.8 %copy.15 = bf16[1,128,2048]{2,1,0:T(8,128)(2,1)} copy(bf16[1,128,2048]{2,1,0:T(8,128)(2,1)S(1)} %bitcast.10) | data formatting | bytes 1048576
  66.6 0.8 %copy.16 = bf16[1,128,2048]{2,1,0:T(8,128)(2,1)} copy(bf16[1,128,2048]{2,1,0:T(8,128)(2,1)S(1)} %bitcast.9) | data formatting | bytes 1048576
  67.4 0.8 %copy.17 = bf16[1,128,2048]{2,1,0:T(8,128)(2,1)} copy(bf16[1,128,2048]{2,1,0:T(8,128)(2,1)S(1)} %bitcast.8) | data formatting | bytes 1048576
  68.2 0.8 %copy.18 = f32[128,1024]{1,0:T(8,128)} copy(f32[128,1024]{1,0:T(8,128)S(1)} %get-tuple-element.19) | data formatting | bytes 1048576
Async XLA Ops:
  1.3 1.0 %copy-start = (bf16[1,128,2048]{2,1,0:T(8,128)(2,1)S(1)}, bf16[1,128,2048]{2,1,0:T(8,128)(2,1)}, u32[]{:S(2)}) copy-start(bf16[1,128,2048]{2,1,0:T(8,128)(2,1)} %param.6) | copy-start | bytes 1572868
  2.3 1.0 %copy-start.1 = (bf16[1,128,2048]{2,1,0:T(8,128)(2,1)S(1)}, bf16[1,128,2048]{2,1,0:T(8,128)(2,1)}, u32[]{:S(2)}) copy-start(bf16[1,128,2048]{2,1,0:T(8,128)(2,1)} %param.7) | copy-start | bytes 1572868
  3.4 1.0 %copy-start.2 = (bf16[1,128,2048]{2,1,0:T(8,128)(2,1)S(1)}, bf16[1,128,2048]{2,1,0:T(8,128)(2,1)}, u32[]{:S(2)}) copy-start(bf16[1,128,2048]{2,1,0:T(8,128)(2,1)} %param.8) | copy-start | bytes 1572868
  4.4 1.0 %copy-start.3 = (bf16[1,128,2048]{2,1,0:T(8,128)(2,1)S(1)}, bf16[1,128,2048]{2,1,0:T(8,128)(2,1)}, u32[]{:S(2)}) copy-start(bf16[1,128,2048]{2,1,0:T(8,128)(2,1)} %param.9) | copy-start | bytes 1572868
  5.4 1.0 %copy-start.4 = (bf16[1,128,2048]{2,1,0:T(8,128)(2,1)S(1)}, bf16[1,128,2048]{2,1,0:T(8,128)(2,1)}, u32[]{:S(2)}) copy-start(bf16[1,128,2048]{2,1,0:T(8,128)(2,1)} %param.10) | copy-start | bytes 1572868

commit v2 on v1

--- a/solution.py
+++ b/solution.py
@@ -206,6 +206,7 @@
 
 HEADS_PER_CHUNK = 2
 CHUNK = HEADS_PER_CHUNK * HEAD_DIM
+VMEM_LIMIT = 63 * 1024 * 1024
 MESH = pl.DeviceIdType.MESH
 F32 = jnp.float32
 BF16 = jnp.bfloat16
@@ -502,6 +503,15 @@
             copy.wait()
 
 
+def store_kernel(a, b, c, d, a_out, b_out, c_out, d_out, sems):
+    pairs = ((a, a_out), (b, b_out), (c, c_out), (d, d_out))
+    copies = [pltpu.make_async_copy(i, o, sems.at[n]) for n, (i, o) in enumerate(pairs)]
+    for copy in copies:
+        copy.start()
+    for copy in copies:
+        copy.wait()
+
+
 def fused_body(layer_input, queries, key_states, value_states, out_grad, block_kinds):
     rows, width = queries.shape[1:]
     half = width // 2
@@ -544,7 +554,7 @@
             dma((chunks,)),
         ],
         compiler_params=pltpu.CompilerParams(
-            collective_id=0, has_side_effects=True, vmem_limit_bytes=48 * 1024 * 1024
+            collective_id=0, has_side_effects=True, vmem_limit_bytes=VMEM_LIMIT
         ),
         cost_estimate=pl.CostEstimate(
             flops=2 * (5 * seq * seq * half + depth * nz * each * half),
@@ -552,6 +562,15 @@
             transcendentals=seq * seq * half // HEAD_DIM,
         ),
     )(block_kinds, layer_input[0], queries[0], key_states[0], value_states[0], out_grad[0])
+    outs = pl.pallas_call(
+        store_kernel,
+        out_shape=tuple(jax.ShapeDtypeStruct(o.shape, o.dtype) for o in outs),
+        in_specs=[pl.BlockSpec(memory_space=pltpu.VMEM)] * 4,
+        out_specs=[pl.BlockSpec(memory_space=pl.ANY)] * 4,
+        scratch_shapes=[dma((4,))],
+        compiler_params=pltpu.CompilerParams(vmem_limit_bytes=VMEM_LIMIT),
+        cost_estimate=pl.CostEstimate(flops=0, bytes_accessed=8 * rows * width * 2, transcendentals=0),
+    )(*outs)
     return (outs[0][None], outs[1][None], outs[2][None], outs[3])
 
 

time: 69.4 us -> 64.1 us (0.924)
  local copies, waits for them, and re-layouts: 8.37 us -> 0 us
  Pallas kernels: 59.3 us -> 62.6 us
    unnamed x14 -> x0, local copies, waits for them, and re-layouts: 8.37 us -> none
    pallas_call x0 -> x1, Pallas kernels: none -> 2.86 us  [fused_body(): pl.pallas_call(store_kernel, out_shape=tuple((jax.ShapeDtypeStruct(o.shap...]
where the time goes in v2:
time: 64.1 us; the launch traced here: 63.9 us
  Pallas kernels  62.6 us (98%)
  between operations  1.29 us (2%)
    pallas_call x1, Pallas kernels, fused_body(): pl.pallas_call(functools.partial(fused_kernel, (rows, half, nz, chunks)),...  59.8 us
    pallas_call x1, Pallas kernels, fused_body(): pl.pallas_call(store_kernel, out_shape=tuple((jax.ShapeDtypeStruct(o.shap...  2.86 us

profile of v2, /device:TPU:0, one launch (start us, length us, event | category | flops | bytes accessed | tf_op | source)
XLA Modules:
  0.0 63.9 jit_solution(14942232999030006769)
XLA Ops:
  1.3 59.8 %shard_map.93 = (bf16[128,2048]{1,0:T(8,128)(2,1)}, bf16[128,2048]{1,0:T(8,128)(2,1)}, bf16[128,2048]{1,0:T(8,128)(2,1)}, f32[128,1024]{1,0:T(8,128)}) custom-call(s32[1,1]{1,0:T(1,128)S(6)} %copy.10.kinds, bf16[128,2048]{1,0:T(8,128)(2,1)} %bitcast.8, bf16[128,2048]{1,0:T(8,128)(2,1)} %bitcast.9, bf16[128,2048]{1,0:T(8,128)(2,1)} %bitcast.10, ...), custom_call_target="tpu_custom_call" | custom-call | flops 1744830464 | bytes 4718592 | tf_op jit(solution)/shard_map/pallas_call | solution.py:525
  61.0 2.9 %shard_map.94 = (bf16[128,2048]{1,0:T(8,128)(2,1)}, bf16[128,2048]{1,0:T(8,128)(2,1)}, bf16[128,2048]{1,0:T(8,128)(2,1)}, f32[128,1024]{1,0:T(8,128)}) custom-call(bf16[128,2048]{1,0:T(8,128)(2,1)} %get-tuple-element.12.a, bf16[128,2048]{1,0:T(8,128)(2,1)} %get-tuple-element.13.b, bf16[128,2048]{1,0:T(8,128)(2,1)} %get-tuple-element.14.c, ...), custom_call_target="tpu_custom_call" | custom-call | bytes 4194304 | tf_op jit(solution)/shard_map/pallas_call | solution.py:565

commit v3 on v2

--- a/solution.py
+++ b/solution.py
@@ -503,12 +503,21 @@
             copy.wait()
 
 
-def store_kernel(a, b, c, d, a_out, b_out, c_out, d_out, sems):
-    pairs = ((a, a_out), (b, b_out), (c, c_out), (d, d_out))
-    copies = [pltpu.make_async_copy(i, o, sems.at[n]) for n, (i, o) in enumerate(pairs)]
-    for copy in copies:
+def store_kernel(a, b, c, d, a_out, b_out, c_out, d_out, a_s, b_s, c_s, d_s, load, store):
+    stages = ((a, a_s, a_out), (b, b_s, b_out), (c, c_s, c_out), (d, d_s, d_out))
+    loads, stores = [], []
+    for n, (src, mid, dst) in enumerate(stages):
+        part = src.shape[0] // 2
+        for p in range(2):
+            piece = pl.ds(p * part, part)
+            loads.append(pltpu.make_async_copy(src.at[piece], mid.at[piece], load.at[n, p]))
+            stores.append(pltpu.make_async_copy(mid.at[piece], dst.at[piece], store.at[n, p]))
+    for copy in loads:
         copy.start()
-    for copy in copies:
+    for copy_in, copy_out in zip(loads, stores):
+        copy_in.wait()
+        copy_out.start()
+    for copy in stores:
         copy.wait()
 
 
@@ -565,9 +574,9 @@
     outs = pl.pallas_call(
         store_kernel,
         out_shape=tuple(jax.ShapeDtypeStruct(o.shape, o.dtype) for o in outs),
-        in_specs=[pl.BlockSpec(memory_space=pltpu.VMEM)] * 4,
+        in_specs=[pl.BlockSpec(memory_space=pl.ANY)] * 4,
         out_specs=[pl.BlockSpec(memory_space=pl.ANY)] * 4,
-        scratch_shapes=[dma((4,))],
+        scratch_shapes=[pltpu.VMEM(o.shape, o.dtype) for o in outs] + [dma((4, 2))] * 2,
         compiler_params=pltpu.CompilerParams(vmem_limit_bytes=VMEM_LIMIT),
         cost_estimate=pl.CostEstimate(flops=0, bytes_accessed=8 * rows * width * 2, transcendentals=0),
     )(*outs)

time: 64.1 us -> 63.6 us (level)
  no operation moved by 1% of the time
where the time goes in v3:
time: 63.6 us; the launch traced here: 63.4 us
  Pallas kernels  62.1 us (98%)
  between operations  1.29 us (2%)
    pallas_call x1, Pallas kernels, fused_body(): pl.pallas_call(functools.partial(fused_kernel, (rows, half, nz, chunks)),...  59.8 us
    pallas_call x1, Pallas kernels, fused_body(): pl.pallas_call(store_kernel, out_shape=tuple((jax.ShapeDtypeStruct(o.shap...  2.4 us

profile of v3, /device:TPU:0, one launch (start us, length us, event | category | flops | bytes accessed | tf_op | source)
XLA Modules:
  0.0 63.4 jit_solution(8844398848757394464)
XLA Ops:
  1.3 59.8 %shard_map.93 = (bf16[128,2048]{1,0:T(8,128)(2,1)}, bf16[128,2048]{1,0:T(8,128)(2,1)}, bf16[128,2048]{1,0:T(8,128)(2,1)}, f32[128,1024]{1,0:T(8,128)}) custom-call(s32[1,1]{1,0:T(1,128)S(6)} %copy.10.kinds, bf16[128,2048]{1,0:T(8,128)(2,1)} %bitcast.8, bf16[128,2048]{1,0:T(8,128)(2,1)} %bitcast.9, bf16[128,2048]{1,0:T(8,128)(2,1)} %bitcast.10, ...), custom_call_target="tpu_custom_call" | custom-call | flops 1744830464 | bytes 4718592 | tf_op jit(solution)/shard_map/pallas_call | solution.py:534
  61.0 2.4 %shard_map.94 = (bf16[128,2048]{1,0:T(8,128)(2,1)}, bf16[128,2048]{1,0:T(8,128)(2,1)}, bf16[128,2048]{1,0:T(8,128)(2,1)}, f32[128,1024]{1,0:T(8,128)}) custom-call(bf16[128,2048]{1,0:T(8,128)(2,1)} %get-tuple-element.12.a, bf16[128,2048]{1,0:T(8,128)(2,1)} %get-tuple-element.13.b, bf16[128,2048]{1,0:T(8,128)(2,1)} %get-tuple-element.14.c, ...), custom_call_target="tpu_custom_call" | custom-call | bytes 4194304 | tf_op jit(solution)/shard_map/pallas_call | solution.py:574
